TPU v7x, 256 devices: a whole 4x4x8 slice. The times are simulated.
256 devices in a mesh: dom: 256 (over z, y, x, core).
Axes of the slice: x: 4, y: 4, z: 8, core: 2. Of those that a mesh axis runs over, the one named last changes fastest.
Arguments:
- modal_state: float32 [56, 9, 32768], P(None, None, 'dom'), may hold values from -6 to 6
- inv_size: float32 [32768], P('dom'), may hold values from 0.5 to 2
- time_step: float32 [], replicated, may hold values from 0.24 to 0.3
- stiffness: float32 [3, 56, 56], replicated, may hold values from -3.5 to 3.5
- star_matrices: float32 [3, 9, 9], replicated, may hold values from -1.25 to 1.25
- projection: float32 [4, 21, 56], replicated, may hold values from -0.75 to 0.75
- lifting: float32 [4, 56, 21], replicated, may hold values from -1.25 to 1.25
- upwind: float32 [9, 9], replicated, may hold values from -2 to 2
- nb_index: int32 [4, 32768], P(None, 'dom'), may hold values from 0 to 255, as said below
- nb_face: int32 [4, 32768], P(None, 'dom'), may hold values from 0 to 3
- iface_elem: int32 [8192], P('dom'), may hold values from 0 to 127
- iface_face: int32 [8192], P('dom'), may hold values from 0 to 3
- iface_counts: int32 [256], replicated, may hold values from 0 to 32
Outputs:
- updated_state: float32 [56, 9, 32768], P(None, None, 'dom')
Inputs may be any that keep to these rules, and one draw needn't show every extreme that they name: nb_index - 64 is the neighbour's offset from the partition's first element; neighbours lie in the same partition or in the adjacent one of the same cluster, never beyond the first or last partition.
All inputs are finite; a program needn't handle non-finite values.
Results may differ from a plain program's by a relative error of at most 0.0001.
Values sent between devices are 32-bit elements; how exact they have to be, the bound alone decides.
No kernel may reach another device: no remote copies, remote signals or barrier semaphores. Data moves between devices by JAX's collectives and lax.ppermute only.
A program may use at most 128 MiB of HBM per device.

v0:
```python
import functools

import jax
import jax.numpy as jnp
from jax import lax
from jax.experimental import pallas as pl
from jax.experimental.pallas import tpu as pltpu
from jax.sharding import PartitionSpec as P

TAYLOR = 6
SUBSTEPS = 4
MODES = 56
QTY = 9
FACE_MODES = 21
FACE_PAD = 24
FACES = 4
CELLS = 128
HALF = 64
SLOTS = 32
WIDTH = QTY * CELLS
FINE = 85
FIRST_PARTNER = 256 - FINE
DENSE = 512
PACKED = (56, CELLS)
LOADED = 12

F32 = jnp.float32
BF16 = jnp.bfloat16


def lanes(q, count=1):
    return slice(q * CELLS, (q + count) * CELLS)


def lane_ids(rows):
    return lax.broadcasted_iota(jnp.int32, (rows, CELLS), 1)


def swap_halves(x):
    return pltpu.roll(x, HALF, 1)


def coarse_part(x):
    return x.astype(BF16).astype(F32)


def field_k(x):
    padded = jnp.concatenate([x, jnp.zeros((8, x.shape[1]), F32)], axis=0)
    hi = padded.astype(BF16)
    lo = (padded - hi.astype(F32)).astype(BF16)
    return jnp.concatenate([hi, lo, hi], axis=0)


def dot(a, b):
    return jnp.dot(a, b, preferred_element_type=F32)


def apply_k(weights, field_ref, out_ref, rows):
    for start in range(0, QTY, 2):
        part = lanes(start, min(2, QTY - start))
        out_ref[:rows, part] = dot(weights, field_k(field_ref[:, part]))


def spread_upwind(upwind_ref, table_ref):
    entries = upwind_ref[...]
    for p in range(QTY):
        table_ref[p * 16 : p * 16 + QTY, :] = jnp.broadcast_to(
            entries[:, p : p + 1], (QTY, CELLS)
        )


def mix_upwind(table_ref, w_of, emit):
    for base in range(0, QTY, 3):
        sums = [None] * 3
        for p in range(QTY):
            w = w_of(p)
            for j in range(3):
                row = p * 16 + base + j
                term = table_ref[row : row + 1, :] * w
                sums[j] = term if sums[j] is None else sums[j] + term
        for j in range(3):
            emit(base + j, sums[j])


def put_dense(value, base, out_ref):
    rows = value.shape[0]
    hi = value.astype(BF16)
    out_ref[base : base + rows, :] = hi
    out_ref[DENSE + base : DENSE + base + rows, :] = (value - hi.astype(F32)).astype(BF16)


def put_scales(star_ref, out_ref):
    wide = lax.broadcasted_iota(jnp.int32, (QTY, DENSE), 1)
    for d in range(3):
        entries = star_ref[:, d, :]
        scale = jnp.zeros((QTY, DENSE), F32)
        for p in range(QTY):
            here = (wide >= p * MODES) & (wide < (p + 1) * MODES)
            scale = jnp.where(here, entries[:, p : p + 1], scale)
        out_ref[16 * d : 16 * d + QTY, :] = scale


def build_dense(scales_ref, blocks, out_ref):
    tiled = []
    for d in range(3):
        columns = []
        for c in range(DENSE // CELLS):
            column = lane_ids(MODES) + c * CELLS
            columns.append(jnp.take_along_axis(blocks[d], column % MODES, axis=1))
        tiled.append(jnp.concatenate(columns, axis=1))

    def rows(q):
        return sum(scales_ref[16 * d + q : 16 * d + q + 1, :] * tiled[d] for d in range(3))

    for q in range(0, QTY - 1, 2):
        put_dense(jnp.concatenate([rows(q), rows(q + 1)], axis=0), q * MODES, out_ref)
    tail = jnp.concatenate([rows(QTY - 1), jnp.zeros((8, DENSE), F32)], axis=0)
    put_dense(tail, (QTY - 1) * MODES, out_ref)


def dense(weights_ref, rows):
    padded = jnp.concatenate([rows, jnp.zeros((8, CELLS), F32)], axis=0)
    hi = padded.astype(BF16)
    lo = (padded - hi.astype(F32)).astype(BF16)
    both = dot(weights_ref[:DENSE, :], jnp.concatenate([hi, lo], axis=1))
    low = dot(weights_ref[DENSE:, :], hi)
    return ((both[:, :CELLS] + both[:, CELLS:]) + low)[: QTY * MODES]


def block(rows, q):
    return rows[q * MODES : (q + 1) * MODES]


def predict_five(dense_ref, v_ref, coef_ref, inv):
    u = coef_ref[TAYLOR - 1 : TAYLOR, :] * v_ref[...]
    for k in range(TAYLOR - 2, -1, -1):
        u = coef_ref[k : k + 1, :] * v_ref[...] - inv * dense(dense_ref, u)
    return u


def predict_three(dense_ref, square_ref, v, coef_ref, inv):
    c = [coef_ref[k : k + 1, :] for k in range(TAYLOR)]
    two = inv * inv
    u = -inv * dense(dense_ref, v)
    top = c[4] * v + c[5] * u
    mid = c[2] * v + c[3] * u + two * dense(square_ref, top)
    return c[0] * v + c[1] * u + two * dense(square_ref, mid)


def fill_coefs(coef_ref, begin, end):
    b, e, fact = begin, end, 1.0
    for k in range(TAYLOR):
        fact = fact * (k + 1)
        coef_ref[k : k + 1, :] = (e - b) * (1.0 / fact)
        b, e = b * begin, e * end


def put_messages(even, u_of, odd_ref, even_ref):
    def put(row, first, second):
        rows = first.shape[0]
        low = lane_ids(rows) < HALF
        turned = swap_halves(second)
        left = jnp.where(low, first, turned)
        right = jnp.where(low, turned, first)
        odd_ref[row : row + rows, :] = jnp.where(even, left, right)
        even_ref[row : row + rows, :] = jnp.where(even, right, left)

    for j in range(QTY // 2):
        put(j * MODES, u_of(2 * j), u_of(2 * j + 1))
    tail = u_of(QTY - 1)
    put(QTY // 2 * MODES, tail[:32], tail[24:])


def take_messages(even, odd_ref, even_ref, halo_ref):
    def take(row, rows):
        low = lane_ids(rows) < HALF
        a, b = odd_ref[row : row + rows, :], even_ref[row : row + rows, :]
        left = jnp.where(even, a, b)
        right = jnp.where(even, b, a)
        first = jnp.where(low, right, left)
        second = swap_halves(jnp.where(low, left, right))
        return first, second

    for j in range(QTY // 2):
        first, second = take(j * MODES, MODES)
        halo_ref[:, lanes(2 * j)] = first
        halo_ref[:, lanes(2 * j + 1)] = second
    first, second = take(QTY // 2 * MODES, 32)
    halo_ref[:32, lanes(QTY - 1)] = first
    halo_ref[32:, lanes(QTY - 1)] = second[8:]


def pick_matrix(target, rows):
    row = lax.broadcasted_iota(jnp.int32, (rows, CELLS), 0)
    return jnp.concatenate(
        [
            jnp.where(row == target[f : f + 1, :], 1.0, 0.0).astype(BF16)
            for f in range(FACES)
        ],
        axis=1,
    )


def slot_matrix(slot_target, live):
    shape = (CELLS, FACES * CELLS)
    row = lax.broadcasted_iota(jnp.int32, shape, 0) % SLOTS
    column = lax.broadcasted_iota(jnp.int32, shape, 1)
    keep = (column == slot_target) & (row.astype(F32) < live)
    return jnp.where(keep, 1.0, 0.0)


def as_column(row):
    shape = (CELLS, CELLS)
    same = lax.broadcasted_iota(jnp.int32, shape, 0) == lax.broadcasted_iota(
        jnp.int32, shape, 1
    )
    kept = jnp.where(same, row.astype(F32), 0.0)
    return jnp.sum(kept, axis=1, keepdims=True).astype(jnp.int32)


def by_quantity(t_ref):
    return jnp.concatenate(
        [
            jnp.concatenate(
                [
                    t_ref[f * FACE_PAD : (f + 1) * FACE_PAD, lanes(q)]
                    for q in range(QTY)
                ],
                axis=0,
            )
            for f in range(FACES)
        ],
        axis=1,
    )


def by_face(g):
    return jnp.concatenate(
        [
            jnp.concatenate(
                [
                    g[q * FACE_PAD : (q + 1) * FACE_PAD, lanes(f)]
                    for f in range(FACES)
                ],
                axis=0,
            )
            for q in range(QTY)
        ],
        axis=1,
    )


def two_parts(x):
    hi = coarse_part(x)
    return jnp.concatenate([hi, x - hi], axis=0).astype(BF16)


def lift(lift_w, stacked):
    both = dot(lift_w, stacked)
    return both[:MODES] + both[MODES:]


def pick_parts(source, matrix):
    return dot(two_parts(source), matrix)


def stack_sums(picked):
    rows = QTY * FACE_PAD
    return two_parts(by_face(picked[:rows] + picked[rows:]))


def stack_parts(picked):
    rows = QTY * FACE_PAD
    return jnp.concatenate([by_face(picked[:rows]), by_face(picked[rows:])], axis=0).astype(BF16)


def pack_slots(tiles, section, out_ref, base):
    whole = jnp.concatenate(tiles + [jnp.zeros((8, CELLS), F32)], axis=0)
    group = lane_ids(8) // SLOTS
    for j in range(whole.shape[0] // 32):
        total = None
        for g in range(4):
            row = 32 * j + 8 * g
            part = whole[row : row + 8]
            if section is not None and g != section:
                part = pltpu.roll(part, SLOTS * ((g - section) % 4), 1)
            total = part if total is None else jnp.where(group == g, part, total)
        out_ref[base + 8 * j : base + 8 * j + 8, :] = total


def unpack_slots(in_ref, base=0):
    group = lane_ids(8) // SLOTS
    tiles = []
    for j in range(QTY * FACE_PAD // 8):
        row = base + 8 * (j // 4)
        tiles.append(jnp.where(group == j % 4, in_ref[row : row + 8, :], 0.0))
    return jnp.concatenate(tiles, axis=0)


def four_times(row):
    return jnp.concatenate([row] * 4, axis=1)


def slot_faces(faces, proj, u_ref, t_ref):
    apply_k(proj, u_ref, t_ref, FACES * FACE_PAD)
    tiles = []
    for q in range(QTY):
        total = jnp.zeros((FACE_PAD, CELLS), F32)
        for f in range(FACES):
            total = jnp.where(
                faces == f, t_ref[f * FACE_PAD : (f + 1) * FACE_PAD, lanes(q)], total
            )
        tiles.append(total)
    return tiles


def live_slots(own, counts_ref):
    fine = own < FINE
    partner = own >= FIRST_PARTNER
    at = jnp.where(fine, own, jnp.where(partner, own - FIRST_PARTNER, -1))
    place = lax.broadcasted_iota(jnp.int32, (2, CELLS), 0) * CELLS + lane_ids(2)
    mine = jnp.where(place == at, counts_ref[...].astype(F32), 0.0)
    return jnp.sum(jnp.sum(mine, axis=1, keepdims=True), axis=0, keepdims=True)


def put_weights_k(value, row, out_ref):
    hi = coarse_part(value)
    rows = slice(row, row + value.shape[0])
    out_ref[rows, 0:MODES] = hi
    out_ref[rows, 64 : 64 + MODES] = hi
    out_ref[rows, 128 : 128 + MODES] = value - hi


def setup_kernel(*refs):
    own_ref, dt_ref, sources, refs = *refs[:2], refs[2 : 2 + LOADED], refs[2 + LOADED :]
    copies, refs = refs[: LOADED - 2], refs[LOADED - 2 :]
    (
        dense_ref, scales_ref, table_ref, early_ref, terms_ref,
        flat_ref, v_ref, u_ref, t_ref, coef_ref, proj_k_ref, star_ref, upwind_ref, done,
    ) = refs
    moves = [
        pltpu.make_async_copy(source, copy, done.at[i])
        for i, (source, copy) in enumerate(zip(sources, (star_ref, *copies, upwind_ref)))
    ]
    for move in moves:
        move.start()
    stiff_ref, state_ref, inv_ref, elem_ref, face_ref, proj_ref = copies[:6]
    for move in moves[:2]:
        move.wait()
    blank = jnp.zeros((MODES, CELLS - MODES), F32)
    blocks = [jnp.concatenate([stiff_ref[d], blank], axis=1) for d in range(3)]
    put_scales(star_ref, scales_ref)
    build_dense(scales_ref, blocks, dense_ref)
    for move in moves[2:]:
        move.wait()
    spread_upwind(upwind_ref, table_ref)

    @pl.when(own_ref[0] >= FIRST_PARTNER)
    def _():
        proj_k_ref[...] = jnp.zeros_like(proj_k_ref)
        for f in range(FACES):
            put_weights_k(proj_ref[:, f, :], f * FACE_PAD, proj_k_ref)
        elems = four_times(elem_ref[...])
        faces = four_times(face_ref[...])
        index = jnp.broadcast_to(elems, (MODES, CELLS))
        for q in range(QTY):
            v_ref[q * MODES : (q + 1) * MODES, :] = jnp.take_along_axis(
                state_ref[q], index, axis=1
            )
        spread = jnp.broadcast_to(inv_ref[...], (8, CELLS))
        inv = jnp.take_along_axis(spread, index[:8], axis=1)[0:1, :]
        section = (lane_ids(1) // SLOTS).astype(F32)
        substep = jnp.full((1, CELLS), dt_ref[0], F32) * (1.0 / SUBSTEPS)
        fill_coefs(coef_ref, section * substep, (section + 1.0) * substep)
        u_ref[...] = predict_five(dense_ref, v_ref, coef_ref, inv)

        def emit(q, value):
            flat_ref[:, lanes(q)] = value

        mix_upwind(table_ref, lambda q: u_ref[q * MODES : (q + 1) * MODES, :], emit)
        tiles = slot_faces(faces, proj_k_ref[...].astype(BF16), flat_ref, t_ref)
        pack_slots(tiles, 0, early_ref, 0)
        pack_slots(tiles, 1, early_ref, PACKED[0])
        for q in range(QTY):
            terms_ref[q * FACE_PAD : (q + 1) * FACE_PAD, :] = tiles[q]


def uniform_coefs(coef_ref, end):
    fill_coefs(coef_ref, jnp.zeros((1, CELLS), F32), jnp.full((1, CELLS), end, F32))


def first_kernel(
    own_ref, dt_ref, table_ref, state_ref, inv_ref, dense_ref,
    flat_ref, w_ref, u_ref, odd_ref, even_ref, v_ref, sum_ref, coef_ref,
):
    own = own_ref[0]
    for q in range(QTY):
        value = state_ref[q]
        v_ref[q * MODES : (q + 1) * MODES, :] = value
        flat_ref[:, lanes(q)] = value
    dt = dt_ref[0]
    uniform_coefs(coef_ref, jnp.where(own < FINE, dt * (1.0 / SUBSTEPS), dt))
    sum_ref[...] = predict_five(dense_ref, v_ref, coef_ref, inv_ref[...])

    def rows(q):
        return sum_ref[q * MODES : (q + 1) * MODES, :]

    def emit(q, value):
        u_ref[:, lanes(q)] = value

    mix_upwind(table_ref, rows, emit)
    put_messages(own % 2 == 0, lambda q: u_ref[:, lanes(q)], odd_ref, even_ref)
    for q in range(QTY):
        w_ref[:, lanes(q)] = rows(q)


def prep_kernel(
    own_ref, counts_ref, dense_ref, scales_ref, stiff_ref, proj_ref, lift_ref, index_ref, face_ref,
    elem_ref, slot_face_ref, terms_ref, square_ref, volume_ref, proj_k_ref, lift_m_ref,
    inside_ref, outside_ref, slots_ref, factor_ref, late_ref, k_ref, m_ref,
):
    own = own_ref[0]

    @pl.when(own < FINE)
    def _():
        whole = dense_ref[...]
        top, low = whole[:DENSE], whole[DENSE:]
        both = dot(whole, top)
        put_dense(both[:DENSE] + (both[DENSE:] + dot(top, low)), 0, square_ref)

    @pl.when(own >= FIRST_PARTNER)
    def _():
        tiles = [terms_ref[q * FACE_PAD : (q + 1) * FACE_PAD, :] for q in range(QTY)]
        pack_slots(tiles, 2, late_ref, 0)
        pack_slots(tiles, 3, late_ref, PACKED[0])

    k_ref[...] = jnp.zeros_like(k_ref)
    for f in range(FACES):
        put_weights_k(proj_ref[:, f, :], f * FACE_PAD, k_ref)
    proj_k_ref[...] = k_ref[...].astype(BF16)
    gap = jnp.zeros((MODES, 64 - MODES), F32)
    pad = jnp.zeros((FACE_PAD - FACE_MODES, MODES), F32)
    tall = jnp.zeros((CELLS - MODES, CELLS), F32)
    one = jnp.concatenate([stiff_ref[0], gap, stiff_ref[1], gap], axis=1)
    one = jnp.concatenate([one, tall], axis=0).T
    faces = [jnp.concatenate([lift_ref[:, f, :], pad], axis=0) for f in range(FACES)]
    faces = jnp.concatenate(faces + [jnp.zeros((CELLS - FACES * FACE_PAD, MODES), F32)], axis=0)
    third = jnp.concatenate([stiff_ref[2], jnp.zeros((CELLS - MODES, MODES), F32)], axis=0)
    side = jnp.zeros((CELLS, 64 - MODES), F32)
    two = jnp.concatenate([faces, side, third, side], axis=1).T
    build_dense(
        scales_ref, [one[:MODES], one[64 : 64 + MODES], two[64 : 64 + MODES]], volume_ref
    )
    value = two[:MODES, : FACES * FACE_PAD]
    hi = coarse_part(value)
    low = value - hi
    m_ref[...] = jnp.concatenate(
        [jnp.concatenate([hi, hi], axis=1), jnp.concatenate([low, low], axis=1)], axis=0
    )
    lift_m_ref[...] = m_ref[...].astype(BF16)
    nb, face = index_ref[...], face_ref[...] * CELLS
    inside = (nb >= HALF) & (nb < HALF + CELLS)
    lane = jnp.where(nb < HALF, nb + HALF, nb - HALF - CELLS)
    inside_ref[...] = pick_matrix(jnp.where(inside, face + nb - HALF, -1), FACES * CELLS)
    outside_ref[...] = pick_matrix(jnp.where(inside, -1, face + lane), FACES * CELLS)
    target = four_times(slot_face_ref[...] * CELLS + elem_ref[...])
    slots = slot_matrix(as_column(target), live_slots(own, counts_ref))
    slots_ref[...] = slots.astype(BF16)
    count = jnp.sum(slots, axis=0, keepdims=True) * 0.25
    factor_ref[...] = jnp.broadcast_to(1.0 + count, factor_ref.shape)


def inner_kernel(
    section, own_ref, state_ref, w_ref, u_ref, inv_ref, inside_ref, factor_ref,
    volume_ref, proj_ref, lift_ref, *rest,
):
    remote_ref, slots_ref = rest[:2]
    out_ref, t_ref = rest[0 if section == 0 else 3 if section == 1 else 2], rest[-1]
    own = own_ref[0]

    def work():
        apply_k(proj_ref[...], u_ref, t_ref, FACES * FACE_PAD)
        own_traces = by_quantity(t_ref)
        if section == 0:
            picked = pick_parts(own_traces, inside_ref[...])
        else:
            remote = unpack_slots(remote_ref, PACKED[0] if section != 2 else 0)
            matrix = jnp.concatenate([inside_ref[...], slots_ref[...]], axis=0)
            picked = pick_parts(jnp.concatenate([own_traces, remote], axis=1), matrix)
        rows = QTY * FACE_PAD
        jump = factor_ref[0:1, :] * own_traces - (picked[:rows] + picked[rows:])
        flux = lift(lift_ref[...], two_parts(by_face(jump)))
        rows = jnp.concatenate([w_ref[:, lanes(q)] for q in range(QTY)], axis=0)
        volume = dense(volume_ref, rows)
        inv = inv_ref[...]
        for q in range(QTY):
            change = block(volume, q) - flux[:, lanes(q)]
            out_ref[:, lanes(q)] = state_ref[:, lanes(q)] + inv * change

    if section == 0:
        work()
    else:
        pl.when(own < FINE)(work)


def halo_lift(
    own, odd_in, even_in, outside_ref, proj_ref, lift_w, halo_ref, t_ref, extra=None
):
    take_messages(own % 2 == 0, odd_in, even_in, halo_ref)
    apply_k(proj_ref[...], halo_ref, t_ref, FACES * FACE_PAD)
    source, matrix = by_quantity(t_ref), outside_ref[...]
    if extra is None:
        return lift(lift_w, stack_parts(pick_parts(source, matrix)))
    source = jnp.concatenate([source, extra[0]], axis=1)
    matrix = jnp.concatenate([matrix, extra[1]], axis=0)
    return lift(lift_w, stack_sums(pick_parts(source, matrix)))


def outer_kernel(
    section, own_ref, dt_ref, table_ref, state_ref, odd_in, even_in, inv_ref, outside_ref,
    proj_ref, lift_ref, dense_ref, square_ref, sum_in, *rest,
):
    flat_ref, w_ref, u_ref, odd_ref, even_ref, sum_ref, halo_ref, t_ref, coef_ref = rest[-9:]
    own = own_ref[0]

    def update():
        extra = None
        if section == 0:
            remote_ref, slots_ref = rest[:2]
            extra = (unpack_slots(remote_ref), slots_ref[...])
        gain = halo_lift(
            own, odd_in, even_in, outside_ref, proj_ref, lift_ref[...], halo_ref, t_ref, extra
        )
        inv = inv_ref[...]
        for q in range(QTY):
            flat_ref[:, lanes(q)] = state_ref[:, lanes(q)] + inv * gain[:, lanes(q)]

    if section == 0:
        update()

    @pl.when(own < FINE)
    def _():
        if section > 0:
            update()
        uniform_coefs(coef_ref, dt_ref[0] * (1.0 / SUBSTEPS))
        rows = jnp.concatenate([flat_ref[:, lanes(q)] for q in range(QTY)], axis=0)
        w = predict_three(dense_ref, square_ref, rows, coef_ref, inv_ref[...])
        for q in range(QTY):
            w_ref[:, lanes(q)] = block(w, q)
        if section == SUBSTEPS - 2:
            elem_ref, slot_face_ref = rest[:2]
            index = jnp.broadcast_to(four_times(elem_ref[...]), (MODES, CELLS))

        def emit(q, value):
            u_ref[:, lanes(q)] = value
            total = sum_in[:, lanes(q)] + value
            if section < SUBSTEPS - 2:
                sum_ref[:, lanes(q)] = total
            else:
                halo_ref[:, lanes(q)] = jnp.take_along_axis(total, index, axis=1)

        mix_upwind(table_ref, lambda q: w_ref[:, lanes(q)], emit)
        put_messages(own % 2 == 0, lambda q: u_ref[:, lanes(q)], odd_ref, even_ref)
        if section == SUBSTEPS - 2:
            faces = four_times(slot_face_ref[...])
            pack_slots(slot_faces(faces, proj_ref[...], halo_ref, t_ref), None, sum_ref, 0)


def last_kernel(
    own_ref, fine_ref, coarse_ref, odd_in, even_in, inv_ref, outside_ref, proj_ref,
    lift_ref, up_ref, slots_ref, out_ref, halo_ref, t_ref, rows_ref, done,
):
    own = own_ref[0]
    inv = inv_ref[...]

    def write(base_ref, stacked):
        moves = []
        for start in range(0, QTY, 2):
            count = min(2, QTY - start)
            gain = lift(lift_ref[...], stacked[:, lanes(start, count)])
            for q in range(start, start + count):
                part = gain[:, lanes(q - start)]
                rows_ref[q] = base_ref[:, lanes(q)] + inv * part
                moves.append(
                    pltpu.make_async_copy(rows_ref.at[q], out_ref.at[q], done.at[q])
                )
                moves[q].start()
        for move in moves:
            move.wait()

    @pl.when(own < FINE)
    def _():
        take_messages(own % 2 == 0, odd_in, even_in, halo_ref)
        apply_k(proj_ref[...], halo_ref, t_ref, FACES * FACE_PAD)
        picked = pick_parts(by_quantity(t_ref), outside_ref[...])
        write(fine_ref, stack_parts(picked))

    @pl.when(own >= FINE)
    def _():
        picked = pick_parts(unpack_slots(up_ref), slots_ref[...])
        write(coarse_ref, stack_sums(picked))


S = pl.BlockSpec(memory_space=pltpu.SMEM)
V = pl.BlockSpec(memory_space=pltpu.VMEM)
H = pl.BlockSpec(memory_space=pltpu.HBM)
FIELD = (MODES, WIDTH)
ROWS = (QTY * MODES, CELLS)
MESSAGE = (256, CELLS)


def call(kernel, inputs, outs, scratch, operands, flops, name, aliases=None, place=None, scalars=2, out_place=V):
    shapes = [
        jax.ShapeDtypeStruct(o, F32) if isinstance(o, tuple) else o for o in outs
    ]
    return pl.pallas_call(
        kernel,
        in_specs=[S] * scalars + [place or V] * (inputs - scalars),
        out_specs=[out_place] * len(outs),
        out_shape=shapes,
        scratch_shapes=[
            pltpu.VMEM(s, F32) if isinstance(s, tuple) else s for s in scratch
        ],
        input_output_aliases=aliases or {},
        compiler_params=pltpu.CompilerParams(vmem_limit_bytes=16 * 1024 * 1024),
        cost_estimate=pl.CostEstimate(
            flops=flops, bytes_accessed=2_000_000, transcendentals=0
        ),
        name=name,
    )(*operands)


def half(*shape):
    return jax.ShapeDtypeStruct(shape, BF16)


def shards(
    modal_state, inv_size, time_step, stiffness, star_matrices, projection, lifting, upwind,
    nb_index, nb_face, iface_elem, iface_face, iface_counts,
):
    own = lax.axis_index("dom").astype(jnp.int32).reshape(1)
    state = modal_state.transpose(1, 0, 2)
    star = star_matrices.transpose(1, 0, 2)
    proj = projection.transpose(1, 0, 2)
    lift_w = lifting.transpose(2, 0, 1)
    dt = time_step.reshape(1)
    inv = inv_size.reshape(1, CELLS)
    elems = iface_elem.reshape(1, SLOTS)
    faces = iface_face.reshape(1, SLOTS)
    counts = iface_counts.reshape(2, CELLS)

    count = lax.axis_size("dom")
    down = [(i + FIRST_PARTNER, i) for i in range(FINE)]
    up = [(i, i + FIRST_PARTNER) for i in range(FINE)]

    def swaps(first, last):
        pairs = [(i, i + 1) for i in range(first, last, 2)]
        pairs = [p for p in pairs if p[1] < last]
        return pairs + [(b, a) for a, b in pairs]

    odd_fine, even_fine = swaps(1, FINE), swaps(0, FINE)
    odd_all = odd_fine + swaps(FINE, count)
    even_all = even_fine + swaps(FINE + 1, count)

    coef = (8, CELLS)
    t_rows = FACES * FACE_PAD
    t_shape = (t_rows, WIDTH)
    wide_operator = (2 * DENSE, DENSE)
    columns = FACES * CELLS

    loaded = (star, stiffness, state, inv, elems, faces, proj, lift_w, nb_index, nb_face,
              counts, upwind)
    *copies, dense_op, scales, table, early, terms = call(
        setup_kernel,
        2 + LOADED,
        [jax.ShapeDtypeStruct(x.shape, x.dtype) for x in loaded[1:-1]]
        + [half(*wide_operator), (48, DENSE), (QTY * 16, CELLS)]
        + [(2 * PACKED[0], CELLS), (QTY * FACE_PAD, CELLS)],
        [FIELD, ROWS, ROWS, t_shape, coef, (t_rows, 192), (QTY, 3, QTY), (QTY, QTY),
         pltpu.SemaphoreType.DMA((LOADED,))],
        (own, dt, *(pltpu.with_memory_space_constraint(x, pltpu.HBM) for x in loaded)),
        20_000_000,
        "setup",
        place=H,
    )
    stiffness, state, inv, elems, faces, proj, lift_w, nb_index, nb_face, counts = copies
    early = lax.ppermute(early, "dom", down)

    flat, w, u, odd, even = call(
        first_kernel,
        6,
        [FIELD, FIELD, FIELD, MESSAGE, MESSAGE],
        [ROWS, ROWS, coef],
        (own, dt, table, state, inv, dense_op),
        2_000_000_000,
        "first",
    )
    total = u
    coarse = None
    for section in range(SUBSTEPS):
        odd_in = lax.ppermute(odd, "dom", odd_all if section == 0 else odd_fine)
        even_in = lax.ppermute(even, "dom", even_all if section == 0 else even_fine)
        if section == 0:
            (
                square_op, volume, proj_k, lift_m, inside, outside, slots, factor,
                late,
            ) = call(
                prep_kernel,
                12,
                [
                    half(*wide_operator), half(*wide_operator), half(t_rows, 192),
                    half(2 * MODES, 2 * t_rows), half(columns, columns),
                    half(columns, columns), half(CELLS, columns), (8, columns),
                    (2 * PACKED[0], CELLS),
                ],
                [(t_rows, 192), (2 * MODES, 2 * t_rows)],
                (own, counts, dense_op, scales, stiffness, proj, lift_w, nb_index, nb_face,
                 elems, faces, terms),
                2_000_000_000,
                "prep",
                scalars=1,
            )
        if section == SUBSTEPS - 1:
            arrived = lax.ppermute(total, "dom", up)
        passed = section == 1
        extra = (() if section == 0 else (early if section == 1 else late, slots))
        results = call(
            functools.partial(inner_kernel, section),
            10 + len(extra) + passed,
            [FIELD] + [(2 * PACKED[0], CELLS)] * passed,
            [t_shape],
            (own, flat, w, u, inv, inside, factor, volume, proj_k, lift_m)
            + extra + (late,) * passed,
            2_000_000_000,
            f"inner{section}",
            {12: 1} if passed else None,
            scalars=1,
        )
        inner = results[0]
        if passed:
            late = lax.ppermute(results[1], "dom", down)
        if section == SUBSTEPS - 1:
            break
        extra = ((early, slots), (), (elems, faces))[section]
        flat, w, u, odd, even, total = call(
            functools.partial(outer_kernel, section),
            13 + len(extra),
            [FIELD, FIELD, FIELD, MESSAGE, MESSAGE,
             FIELD if section < SUBSTEPS - 2 else PACKED],
            [FIELD, t_shape, coef],
            (own, dt, table, inner, odd_in, even_in, inv, outside, proj_k, lift_m, dense_op,
             square_op, total) + extra,
            2_000_000_000,
            f"outer{section}",
        )
        if section == 0:
            coarse = flat
    (out,) = call(
        last_kernel,
        11,
        [pltpu.HBM((QTY, MODES, CELLS), F32)],
        [FIELD, t_shape, (QTY, MODES, CELLS), pltpu.SemaphoreType.DMA((QTY,))],
        (own, inner, coarse, odd_in, even_in, inv, outside, proj_k, lift_m, arrived, slots),
        1_000_000_000,
        "last",
        scalars=1,
        out_place=H,
    )
    return out.transpose(1, 0, 2)


def solution(mesh):
    return jax.shard_map(
        shards,
        mesh=mesh,
        in_specs=(
            P(None, None, "dom"),
            P("dom"),
            P(),
            P(),
            P(),
            P(),
            P(),
            P(),
            P(None, "dom"),
            P(None, "dom"),
            P("dom"),
            P("dom"),
            P(),
        ),
        out_specs=P(None, None, "dom"),
        check_vma=False,
    )
```

profile of v0, /device:TPU:64, one launch (start us, length us, event | category | flops | bytes accessed | tf_op | source)
XLA Modules:
  0.0 59.0 jit_solution(16147844130550120620)
XLA Ops:
  0.7 1.8 %setup.1 = (f32[3,56,56]{2,1,0:T(8,128)S(1)}, f32[9,56,128]{2,1,0:T(8,128)S(1)}, f32[1,128]{1,0:T(1,128)S(1)}, s32[1,32]{1,0:T(1,128)S(1)}, s32[1,32]{1,0:T(1,12...) custom-call(s32[1]{0:T(128)} %bitcast.refs_0_.own_ref, ...), custom_call_target="tpu_custom_call" | custom-call | flops 20000000 | bytes 2000000 | tf_op jit(solution)/shard_map/setup/pallas_call | solution.py:616
  2.5 1.3 %collective-permute-start.2 = (f32[112,128]{1,0:T(8,128)S(1)}, f32[112,128]{1,0:T(8,128)S(1)}, u32[]{:S(2)}, u32[]{:S(2)}) collective-permute-start(f32[112,128]{1,0:T(8,128)S(1)} %get-tuple-element.80), channel_id=1, source_target_pairs={{171,0},{172,1},{173,2},{174,3},{175,4},{176,5},{177,6},{178,7},{1... | collective-permute-start | bytes 172040 | tf_op jit(solution)/shard_map/ppermute | solution.py:687
  3.8 2.0 %first.1 = (f32[56,1152]{1,0:T(8,128)S(1)}, f32[56,1152]{1,0:T(8,128)S(1)}, f32[56,1152]{1,0:T(8,128)S(1)}, f32[256,128]{1,0:T(8,128)S(1)}, f32[256,128]{1,0:T(8,128)S(1)}) custom-call(s32[1]{0:T(128)} %bitcast.refs_0_.own_ref, f32[1]{0:T(128)} %bitcast.12.dt_ref, f32[144,128]{1,0:T(8,128)S(1)} %get-tuple-element.54.table_ref, ...), custom_call_target="tpu_custom_call" | custom-call | flops 2000000000 | bytes 2000000 | tf_op jit(solution)/shard_map/first/pallas_call | solution.py:616
  5.8 6.1 %collective-permute-start = (f32[256,128]{1,0:T(8,128)S(1)}, f32[256,128]{1,0:T(8,128)S(1)}, u32[]{:S(2)}, u32[]{:S(2)}) collective-permute-start(f32[256,128]{1,0:T(8,128)S(1)} %get-tuple-element.76), channel_id=1, source_target_pairs={{1,2},{3,4},{5,6},{7,8},{9,10},{11,12},{13,14},{15,16},{17,18},{19... | collective-permute-start | bytes 393224 | tf_op jit(solution)/shard_map/ppermute | solution.py:701
  11.9 1.9 %collective-permute-start.1 = (f32[256,128]{1,0:T(8,128)S(1)}, f32[256,128]{1,0:T(8,128)S(1)}, u32[]{:S(2)}, u32[]{:S(2)}) collective-permute-start(f32[256,128]{1,0:T(8,128)S(1)} %get-tuple-element.77), channel_id=1, source_target_pairs={{0,1},{2,3},{4,5},{6,7},{8,9},{10,11},{12,13},{14,15},{16,17},{18,... | collective-permute-start | bytes 393224 | tf_op jit(solution)/shard_map/ppermute | solution.py:702
  13.8 2.0 %prep.1 = (bf16[1024,512]{1,0:T(8,128)(2,1)S(1)}, bf16[1024,512]{1,0:T(8,128)(2,1)S(1)}, bf16[96,192]{1,0:T(8,128)(2,1)S(1)}, bf16[112,192]{1,0:T(8,128)(2,1)S(1...) custom-call(s32[1]{0:T(128)} %bitcast.refs_0_.own_ref, ...), custom_call_target="tpu_custom_call" | custom-call | flops 2000000000 | bytes 2000000 | tf_op jit(solution)/shard_map/prep/pallas_call | solution.py:616
  15.9 1.0 %inner0.1.state_ref = f32[56,1152]{1,0:T(8,128)S(1)} custom-call(s32[1]{0:T(128)} %bitcast.refs_0_.own_ref, f32[56,1152]{1,0:T(8,128)S(1)} %get-tuple-element.58.state_ref, f32[56,1152]{1,0:T(8,128)S(1)} %get-tuple-element.59.w_ref, f32[56,1152]{1,0:T(8,128)S(1)} %get-tuple-element.60.u_ref.sum_in, f32[1,128]{1,0:T(1,128)S(1)} %get-tuple-element.56.inv_ref, ...), custom_call_target="tpu_custom_call" | custom-call | flops 2000000000 | bytes 2000000 | tf_op jit(solution)/shard_map/inner0/pallas_call | solution.py:616
  16.9 2.2 %outer0.1 = (f32[56,1152]{1,0:T(8,128)S(1)}, f32[56,1152]{1,0:T(8,128)S(1)}, f32[56,1152]{1,0:T(8,128)S(1)}, f32[256,128]{1,0:T(8,128)S(1)}, f32[256,128]{1,0:T(8,128)S(1)}, /*index=5*/f32[56,1152]{1,0:T(8,128)S(1)}) custom-call(s32[1]{0:T(128)} %bitcast.refs_0_.own_ref, f32[1]{0:T(128)} %bitcast.13.dt_ref, f32[144,128]{1,0:T(8,128)S(1)} %get-tuple-element.54.table_ref, ...), custom_call_target="tpu_custom_call" | custom-call | flops 2000000000 | bytes 2000000 | tf_op jit(solution)/shard_map/outer0/pallas_call | solution.py:616
  19.2 6.8 %collective-permute-start.3 = (f32[256,128]{1,0:T(8,128)S(1)}, f32[256,128]{1,0:T(8,128)S(1)}, u32[]{:S(2)}, u32[]{:S(2)}) collective-permute-start(f32[256,128]{1,0:T(8,128)S(1)} %get-tuple-element.87), channel_id=1, source_target_pairs={{1,2},{3,4},{5,6},{7,8},{9,10},{11,12},{13,14},{15,16},{17,18},{19... | collective-permute-start | bytes 393224 | tf_op jit(solution)/shard_map/ppermute | solution.py:701
  26.0 1.9 %collective-permute-start.4 = (f32[256,128]{1,0:T(8,128)S(1)}, f32[256,128]{1,0:T(8,128)S(1)}, u32[]{:S(2)}, u32[]{:S(2)}) collective-permute-start(f32[256,128]{1,0:T(8,128)S(1)} %get-tuple-element.88), channel_id=1, source_target_pairs={{0,1},{2,3},{4,5},{6,7},{8,9},{10,11},{12,13},{14,15},{16,17},{18,... | collective-permute-start | bytes 393224 | tf_op jit(solution)/shard_map/ppermute | solution.py:702
  27.9 1.1 %inner1.1 = (f32[56,1152]{1,0:T(8,128)S(1)}, f32[112,128]{1,0:T(8,128)S(1)}) custom-call(s32[1]{0:T(128)} %bitcast.refs_0_.own_ref, f32[56,1152]{1,0:T(8,128)S(1)} %get-tuple-element.82.state_ref.coarse_ref, f32[56,1152]{1,0:T(8,128)S(1)} %get-tuple-element.83.w_ref, f32[56,1152]{1,0:T(8,128)S(1)} %get-tuple-element.84.u_ref, ...), custom_call_target="tpu_custom_call", output_to_operand_aliasing={{1}: (12, {})} | custom-call | flops 2000000000 | bytes 2000000 | tf_op jit(solution)/shard_map/inner1/pallas_call | solution.py:616
  29.1 1.3 %collective-permute-start.5 = (f32[112,128]{1,0:T(8,128)S(1)}, f32[112,128]{1,0:T(8,128)S(1)}, u32[]{:S(2)}, u32[]{:S(2)}) collective-permute-start(f32[112,128]{1,0:T(8,128)S(1)} %get-tuple-element.93), channel_id=1, source_target_pairs={{171,0},{172,1},{173,2},{174,3},{175,4},{176,5},{177,6},{178,7},{1... | collective-permute-start | bytes 172040 | tf_op jit(solution)/shard_map/ppermute | solution.py:741
  30.4 2.1 %outer1.1 = (f32[56,1152]{1,0:T(8,128)S(1)}, f32[56,1152]{1,0:T(8,128)S(1)}, f32[56,1152]{1,0:T(8,128)S(1)}, f32[256,128]{1,0:T(8,128)S(1)}, f32[256,128]{1,0:T(8,128)S(1)}, /*index=5*/f32[56,1152]{1,0:T(8,128)S(1)}) custom-call(s32[1]{0:T(128)} %bitcast.refs_0_.own_ref, f32[1]{0:T(128)} %bitcast.14.dt_ref, f32[144,128]{1,0:T(8,128)S(1)} %get-tuple-element.54.table_ref, ...), custom_call_target="tpu_custom_call" | custom-call | flops 2000000000 | bytes 2000000 | tf_op jit(solution)/shard_map/outer1/pallas_call | solution.py:616
  32.5 6.1 %collective-permute-start.6 = (f32[256,128]{1,0:T(8,128)S(1)}, f32[256,128]{1,0:T(8,128)S(1)}, u32[]{:S(2)}, u32[]{:S(2)}) collective-permute-start(f32[256,128]{1,0:T(8,128)S(1)} %get-tuple-element.94), channel_id=1, source_target_pairs={{1,2},{3,4},{5,6},{7,8},{9,10},{11,12},{13,14},{15,16},{17,18},{19... | collective-permute-start | bytes 393224 | tf_op jit(solution)/shard_map/ppermute | solution.py:701
  38.6 1.9 %collective-permute-start.7 = (f32[256,128]{1,0:T(8,128)S(1)}, f32[256,128]{1,0:T(8,128)S(1)}, u32[]{:S(2)}, u32[]{:S(2)}) collective-permute-start(f32[256,128]{1,0:T(8,128)S(1)} %get-tuple-element.95), channel_id=1, source_target_pairs={{0,1},{2,3},{4,5},{6,7},{8,9},{10,11},{12,13},{14,15},{16,17},{18,... | collective-permute-start | bytes 393224 | tf_op jit(solution)/shard_map/ppermute | solution.py:702
  40.5 1.3 %inner2.1.state_ref = f32[56,1152]{1,0:T(8,128)S(1)} custom-call(s32[1]{0:T(128)} %bitcast.refs_0_.own_ref, f32[56,1152]{1,0:T(8,128)S(1)} %get-tuple-element.90.state_ref, f32[56,1152]{1,0:T(8,128)S(1)} %get-tuple-element.91.w_ref, f32[56,1152]{1,0:T(8,128)S(1)} %get-tuple-element.92.u_ref, f32[1,128]{1,0:T(1,128)S(1)} %get-tuple-element.56.inv_ref, ...), custom_call_target="tpu_custom_call" | custom-call | flops 2000000000 | bytes 2000000 | tf_op jit(solution)/shard_map/inner2/pallas_call | solution.py:616
  41.8 1.4 %collective-permute-done.6.odd_in = f32[256,128]{1,0:T(8,128)S(1)} collective-permute-done((f32[256,128]{1,0:T(8,128)S(1)}, f32[256,128]{1,0:T(8,128)S(1)}, u32[]{:S(2)}, u32[]{:S(2)}) %collective-permute-start.6) | collective-permute-done | bytes 131104 | tf_op jit(solution)/shard_map/ppermute | solution.py:701
  43.2 2.3 %outer2.1 = (f32[56,1152]{1,0:T(8,128)S(1)}, f32[56,1152]{1,0:T(8,128)S(1)}, f32[56,1152]{1,0:T(8,128)S(1)}, f32[256,128]{1,0:T(8,128)S(1)}, f32[256,128]{1,0:T(8,128)S(1)}, /*index=5*/f32[56,128]{1,0:T(8,128)S(1)}) custom-call(s32[1]{0:T(128)} %bitcast.refs_0_.own_ref, f32[1]{0:T(128)} %bitcast.15.dt_ref, f32[144,128]{1,0:T(8,128)S(1)} %get-tuple-element.54.table_ref, ...), custom_call_target="tpu_custom_call" | custom-call | flops 2000000000 | bytes 2000000 | tf_op jit(solution)/shard_map/outer2/pallas_call | solution.py:616
  45.5 1.3 %collective-permute-start.10 = (f32[56,128]{1,0:T(8,128)S(1)}, f32[56,128]{1,0:T(8,128)S(1)}, u32[]{:S(2)}, u32[]{:S(2)}) collective-permute-start(f32[56,128]{1,0:T(8,128)S(1)} %get-tuple-element.102), channel_id=1, source_target_pairs={{0,171},{1,172},{2,173},{3,174},{4,175},{5,176},{6,177},{7,178},{8... | collective-permute-start | bytes 86024 | tf_op jit(solution)/shard_map/ppermute | solution.py:724
  46.8 5.8 %collective-permute-start.8 = (f32[256,128]{1,0:T(8,128)S(1)}, f32[256,128]{1,0:T(8,128)S(1)}, u32[]{:S(2)}, u32[]{:S(2)}) collective-permute-start(f32[256,128]{1,0:T(8,128)S(1)} %get-tuple-element.100), channel_id=1, source_target_pairs={{1,2},{3,4},{5,6},{7,8},{9,10},{11,12},{13,14},{15,16},{17,18},{19... | collective-permute-start | bytes 393224 | tf_op jit(solution)/shard_map/ppermute | solution.py:701
  52.6 1.9 %collective-permute-start.9 = (f32[256,128]{1,0:T(8,128)S(1)}, f32[256,128]{1,0:T(8,128)S(1)}, u32[]{:S(2)}, u32[]{:S(2)}) collective-permute-start(f32[256,128]{1,0:T(8,128)S(1)} %get-tuple-element.101), channel_id=1, source_target_pairs={{0,1},{2,3},{4,5},{6,7},{8,9},{10,11},{12,13},{14,15},{16,17},{18,... | collective-permute-start | bytes 393224 | tf_op jit(solution)/shard_map/ppermute | solution.py:702
  54.6 1.2 %inner3.1.fine_ref = f32[56,1152]{1,0:T(8,128)S(1)} custom-call(s32[1]{0:T(128)} %bitcast.refs_0_.own_ref, f32[56,1152]{1,0:T(8,128)S(1)} %get-tuple-element.97.state_ref, f32[56,1152]{1,0:T(8,128)S(1)} %get-tuple-element.98.w_ref, f32[56,1152]{1,0:T(8,128)S(1)} %get-tuple-element.99.u_ref, f32[1,128]{1,0:T(1,128)S(1)} %get-tuple-element.56.inv_ref, ...), custom_call_target="tpu_custom_call" | custom-call | flops 2000000000 | bytes 2000000 | tf_op jit(solution)/shard_map/inner3/pallas_call | solution.py:616
  55.7 1.6 %collective-permute-done.8.odd_in = f32[256,128]{1,0:T(8,128)S(1)} collective-permute-done((f32[256,128]{1,0:T(8,128)S(1)}, f32[256,128]{1,0:T(8,128)S(1)}, u32[]{:S(2)}, u32[]{:S(2)}) %collective-permute-start.8) | collective-permute-done | bytes 131104 | tf_op jit(solution)/shard_map/ppermute | solution.py:701
  57.3 1.5 %last.1 = f32[9,56,128]{2,1,0:T(8,128)} custom-call(s32[1]{0:T(128)} %bitcast.refs_0_.own_ref, f32[56,1152]{1,0:T(8,128)S(1)} %inner3.1.fine_ref, f32[56,1152]{1,0:T(8,128)S(1)} %get-tuple-element.82.state_ref.coarse_ref, f32[256,128]{1,0:T(8,128)S(1)} %collective-permute-done.8.odd_in, f32[256,128]{1,0:T(8,128)S(1)} %collective-permute-done.9.even_in, ...), custom_call_target="tpu_custom_call" | custom-call | flops 1000000000 | bytes 2000000 | tf_op jit(solution)/shard_map/last/pallas_call | solution.py:616
  (9 shorter events, 0.0 us)
Async XLA Ops:
  2.5 14.4 %collective-permute-start.2 = (f32[112,128]{1,0:T(8,128)S(1)}, f32[112,128]{1,0:T(8,128)S(1)}, u32[]{:S(2)}, u32[]{:S(2)}) collective-permute-start(f32[112,128]{1,0:T(8,128)S(1)} %get-tuple-element.80), channel_id=1, source_target_pairs={{171,0},{172,1},{173,2},{174,3},{175,4},{176,5},{177,6},{178,7},{1... | collective-permute-start | bytes 172040 | tf_op jit(solution)/shard_map/ppermute | solution.py:687
  5.8 11.1 %collective-permute-start = (f32[256,128]{1,0:T(8,128)S(1)}, f32[256,128]{1,0:T(8,128)S(1)}, u32[]{:S(2)}, u32[]{:S(2)}) collective-permute-start(f32[256,128]{1,0:T(8,128)S(1)} %get-tuple-element.76), channel_id=1, source_target_pairs={{1,2},{3,4},{5,6},{7,8},{9,10},{11,12},{13,14},{15,16},{17,18},{19... | collective-permute-start | bytes 393224 | tf_op jit(solution)/shard_map/ppermute | solution.py:701
  11.9 5.0 %collective-permute-start.1 = (f32[256,128]{1,0:T(8,128)S(1)}, f32[256,128]{1,0:T(8,128)S(1)}, u32[]{:S(2)}, u32[]{:S(2)}) collective-permute-start(f32[256,128]{1,0:T(8,128)S(1)} %get-tuple-element.77), channel_id=1, source_target_pairs={{0,1},{2,3},{4,5},{6,7},{8,9},{10,11},{12,13},{14,15},{16,17},{18,... | collective-permute-start | bytes 393224 | tf_op jit(solution)/shard_map/ppermute | solution.py:702
  19.2 11.2 %collective-permute-start.3 = (f32[256,128]{1,0:T(8,128)S(1)}, f32[256,128]{1,0:T(8,128)S(1)}, u32[]{:S(2)}, u32[]{:S(2)}) collective-permute-start(f32[256,128]{1,0:T(8,128)S(1)} %get-tuple-element.87), channel_id=1, source_target_pairs={{1,2},{3,4},{5,6},{7,8},{9,10},{11,12},{13,14},{15,16},{17,18},{19... | collective-permute-start | bytes 393224 | tf_op jit(solution)/shard_map/ppermute | solution.py:701
  26.0 4.4 %collective-permute-start.4 = (f32[256,128]{1,0:T(8,128)S(1)}, f32[256,128]{1,0:T(8,128)S(1)}, u32[]{:S(2)}, u32[]{:S(2)}) collective-permute-start(f32[256,128]{1,0:T(8,128)S(1)} %get-tuple-element.88), channel_id=1, source_target_pairs={{0,1},{2,3},{4,5},{6,7},{8,9},{10,11},{12,13},{14,15},{16,17},{18,... | collective-permute-start | bytes 393224 | tf_op jit(solution)/shard_map/ppermute | solution.py:702
  29.1 11.4 %collective-permute-start.5 = (f32[112,128]{1,0:T(8,128)S(1)}, f32[112,128]{1,0:T(8,128)S(1)}, u32[]{:S(2)}, u32[]{:S(2)}) collective-permute-start(f32[112,128]{1,0:T(8,128)S(1)} %get-tuple-element.93), channel_id=1, source_target_pairs={{171,0},{172,1},{173,2},{174,3},{175,4},{176,5},{177,6},{178,7},{1... | collective-permute-start | bytes 172040 | tf_op jit(solution)/shard_map/ppermute | solution.py:741
  32.5 10.8 %collective-permute-start.6 = (f32[256,128]{1,0:T(8,128)S(1)}, f32[256,128]{1,0:T(8,128)S(1)}, u32[]{:S(2)}, u32[]{:S(2)}) collective-permute-start(f32[256,128]{1,0:T(8,128)S(1)} %get-tuple-element.94), channel_id=1, source_target_pairs={{1,2},{3,4},{5,6},{7,8},{9,10},{11,12},{13,14},{15,16},{17,18},{19... | collective-permute-start | bytes 393224 | tf_op jit(solution)/shard_map/ppermute | solution.py:701
  38.6 4.7 %collective-permute-start.7 = (f32[256,128]{1,0:T(8,128)S(1)}, f32[256,128]{1,0:T(8,128)S(1)}, u32[]{:S(2)}, u32[]{:S(2)}) collective-permute-start(f32[256,128]{1,0:T(8,128)S(1)} %get-tuple-element.95), channel_id=1, source_target_pairs={{0,1},{2,3},{4,5},{6,7},{8,9},{10,11},{12,13},{14,15},{16,17},{18,... | collective-permute-start | bytes 393224 | tf_op jit(solution)/shard_map/ppermute | solution.py:702
  45.5 10.2 %collective-permute-start.10 = (f32[56,128]{1,0:T(8,128)S(1)}, f32[56,128]{1,0:T(8,128)S(1)}, u32[]{:S(2)}, u32[]{:S(2)}) collective-permute-start(f32[56,128]{1,0:T(8,128)S(1)} %get-tuple-element.102), channel_id=1, source_target_pairs={{0,171},{1,172},{2,173},{3,174},{4,175},{5,176},{6,177},{7,178},{8... | collective-permute-start | bytes 86024 | tf_op jit(solution)/shard_map/ppermute | solution.py:724
  46.8 10.5 %collective-permute-start.8 = (f32[256,128]{1,0:T(8,128)S(1)}, f32[256,128]{1,0:T(8,128)S(1)}, u32[]{:S(2)}, u32[]{:S(2)}) collective-permute-start(f32[256,128]{1,0:T(8,128)S(1)} %get-tuple-element.100), channel_id=1, source_target_pairs={{1,2},{3,4},{5,6},{7,8},{9,10},{11,12},{13,14},{15,16},{17,18},{19... | collective-permute-start | bytes 393224 | tf_op jit(solution)/shard_map/ppermute | solution.py:701
  52.6 4.7 %collective-permute-start.9 = (f32[256,128]{1,0:T(8,128)S(1)}, f32[256,128]{1,0:T(8,128)S(1)}, u32[]{:S(2)}, u32[]{:S(2)}) collective-permute-start(f32[256,128]{1,0:T(8,128)S(1)} %get-tuple-element.101), channel_id=1, source_target_pairs={{0,1},{2,3},{4,5},{6,7},{8,9},{10,11},{12,13},{14,15},{16,17},{18,... | collective-permute-start | bytes 393224 | tf_op jit(solution)/shard_map/ppermute | solution.py:702
where the time goes:
time: 59.3 us; the launch traced here: 59 us
  starting transfers between devices  36.4 us (61%)
  Pallas kernels  18.6 us (31%)
  waiting for transfers between devices  3.03 us (5%)
  between operations  1.02 us (2%)
    ppermute x4, starting transfers between devices, shards(): odd_in = lax.ppermute(odd, 'dom', odd_all if section == 0 else odd_fine)  24.8 us
    pallas_call x11, Pallas kernels, call(): pl.pallas_call(kernel, in_specs=[S] * scalars + [place or V] * (inputs -...  18.6 us
    ppermute x4, starting transfers between devices, shards(): even_in = lax.ppermute(even, 'dom', even_all if section == 0 else even_fine)  7.68 us
    ppermute x4, waiting for transfers between devices, shards(): odd_in = lax.ppermute(odd, 'dom', odd_all if section == 0 else odd_fine)  3.01 us
    ppermute x1, starting transfers between devices, shards(): early = lax.ppermute(early, 'dom', down)  1.29 us
    ppermute x1, starting transfers between devices, shards(): late = lax.ppermute(results[1], 'dom', down)  1.29 us
    ppermute x1, starting transfers between devices, shards(): arrived = lax.ppermute(total, 'dom', up)  1.29 us
  transfers between devices with their start and end apart: 11, of which 2 were waited for; matrix products, arithmetic and copies ran while one was open for 0% of the time, Pallas kernels for 18%

commit v1 on v0

--- a/solution.py
+++ b/solution.py
@@ -22,7 +22,7 @@
 FIRST_PARTNER = 256 - FINE
 DENSE = 512
 PACKED = (56, CELLS)
-LOADED = 12
+LOADED = 8
 
 F32 = jnp.float32
 BF16 = jnp.bfloat16
@@ -331,32 +331,41 @@
     out_ref[rows, 128 : 128 + MODES] = value - hi
 
 
-def setup_kernel(*refs):
-    own_ref, dt_ref, sources, refs = *refs[:2], refs[2 : 2 + LOADED], refs[2 + LOADED :]
-    copies, refs = refs[: LOADED - 2], refs[LOADED - 2 :]
+def stiffness_blocks(stiff_ref):
+    blank = jnp.zeros((MODES, CELLS - MODES), F32)
+    return [jnp.concatenate([stiff_ref[d], blank], axis=1) for d in range(3)]
+
+
+def setup_kernel(
+    own_ref, star_ref, stiff_ref, upwind_ref, inv_ref, dense_ref, scales_ref, table_ref
+):
+    put_scales(star_ref, scales_ref)
+    build_dense(scales_ref, stiffness_blocks(stiff_ref), dense_ref)
+    spread_upwind(upwind_ref, table_ref)
+
+
+def remote_kernel(own_ref, dt_ref, *refs):
+    sources, (early_ref, terms_ref), refs = refs[:LOADED], refs[LOADED : LOADED + 2], refs[LOADED + 2 :]
+    copies, refs = refs[:LOADED], refs[LOADED:]
     (
-        dense_ref, scales_ref, table_ref, early_ref, terms_ref,
-        flat_ref, v_ref, u_ref, t_ref, coef_ref, proj_k_ref, star_ref, upwind_ref, done,
+        dense_ref, scales_ref, table_ref,
+        flat_ref, v_ref, u_ref, t_ref, coef_ref, proj_k_ref, done,
     ) = refs
-    moves = [
-        pltpu.make_async_copy(source, copy, done.at[i])
-        for i, (source, copy) in enumerate(zip(sources, (star_ref, *copies, upwind_ref)))
-    ]
-    for move in moves:
-        move.start()
-    stiff_ref, state_ref, inv_ref, elem_ref, face_ref, proj_ref = copies[:6]
-    for move in moves[:2]:
-        move.wait()
-    blank = jnp.zeros((MODES, CELLS - MODES), F32)
-    blocks = [jnp.concatenate([stiff_ref[d], blank], axis=1) for d in range(3)]
-    put_scales(star_ref, scales_ref)
-    build_dense(scales_ref, blocks, dense_ref)
-    for move in moves[2:]:
-        move.wait()
-    spread_upwind(upwind_ref, table_ref)
 
     @pl.when(own_ref[0] >= FIRST_PARTNER)
     def _():
+        moves = [
+            pltpu.make_async_copy(source, copy, done.at[i])
+            for i, (source, copy) in enumerate(zip(sources, copies))
+        ]
+        for move in moves:
+            move.start()
+        star_ref, stiff_ref, upwind_ref, state_ref, inv_ref, elem_ref, face_ref, proj_ref = copies
+        for move in moves:
+            move.wait()
+        setup_kernel(
+            own_ref, star_ref, stiff_ref, upwind_ref, inv_ref, dense_ref, scales_ref, table_ref
+        )
         proj_k_ref[...] = jnp.zeros_like(proj_k_ref)
         for f in range(FACES):
             put_weights_k(proj_ref[:, f, :], f * FACE_PAD, proj_k_ref)
@@ -668,23 +677,26 @@
     wide_operator = (2 * DENSE, DENSE)
     columns = FACES * CELLS
 
-    loaded = (star, stiffness, state, inv, elems, faces, proj, lift_w, nb_index, nb_face,
-              counts, upwind)
-    *copies, dense_op, scales, table, early, terms = call(
-        setup_kernel,
+    loaded = (star, stiffness, upwind, state, inv, elems, faces, proj)
+    tables = [half(*wide_operator), (48, DENSE), (QTY * 16, CELLS)]
+    early, terms = call(
+        remote_kernel,
         2 + LOADED,
-        [jax.ShapeDtypeStruct(x.shape, x.dtype) for x in loaded[1:-1]]
-        + [half(*wide_operator), (48, DENSE), (QTY * 16, CELLS)]
-        + [(2 * PACKED[0], CELLS), (QTY * FACE_PAD, CELLS)],
-        [FIELD, ROWS, ROWS, t_shape, coef, (t_rows, 192), (QTY, 3, QTY), (QTY, QTY),
-         pltpu.SemaphoreType.DMA((LOADED,))],
+        [(2 * PACKED[0], CELLS), (QTY * FACE_PAD, CELLS)],
+        [pltpu.VMEM(x.shape, x.dtype) for x in loaded]
+        + [pltpu.VMEM(wide_operator, BF16), (48, DENSE), (QTY * 16, CELLS)]
+        + [FIELD, ROWS, ROWS, t_shape, coef, (t_rows, 192),
+           pltpu.SemaphoreType.DMA((LOADED,))],
         (own, dt, *(pltpu.with_memory_space_constraint(x, pltpu.HBM) for x in loaded)),
         20_000_000,
-        "setup",
+        "remote",
         place=H,
     )
-    stiffness, state, inv, elems, faces, proj, lift_w, nb_index, nb_face, counts = copies
     early = lax.ppermute(early, "dom", down)
+    dense_op, scales, table = call(
+        setup_kernel, 5, tables, [], (own, star, stiffness, upwind, inv), 20_000_000, "setup",
+        scalars=1,
+    )
 
     flat, w, u, odd, even = call(
         first_kernel,

time: 59.3 us -> 58.9 us (level)
  Pallas kernels: 18.6 us -> 17.3 us
  starting transfers between devices: 36.4 us -> 35.5 us
  waiting for transfers between devices: 3.03 us -> 3.89 us
  local copies, waits for them, and re-layouts: 0 us -> 0.67 us
    pallas_call x11 -> x12, Pallas kernels: 18.6 us -> 17.3 us  [call(): pl.pallas_call(kernel, in_specs=[S] * scalars + [place or V] * (inputs -...]
    ppermute x4, starting transfers between devices: 24.8 us -> 23.8 us  [shards(): odd_in = lax.ppermute(odd, 'dom', odd_all if section == 0 else odd_fine)]
    ppermute x4, waiting for transfers between devices: 3.01 us -> 3.85 us  [shards(): odd_in = lax.ppermute(odd, 'dom', odd_all if section == 0 else odd_fine)]
    unnamed x0 -> x24, local copies, waits for them, and re-layouts: none -> 0.67 us
  transfers between devices with their start and end apart: 11 -> 11, of which waited for: 2 -> 2; matrix products, arithmetic and copies ran while one was open for 0% -> 0% of each run, Pallas kernels for 18% -> 19%
where the time goes in v1:
time: 58.9 us; the launch traced here: 58.5 us
  starting transfers between devices  35.5 us (60%)
  Pallas kernels  17.3 us (29%)
  waiting for transfers between devices  3.89 us (7%)
  between operations  1.19 us (2%)
  local copies, waits for them, and re-layouts  0.67 us (1%)
    ppermute x4, starting transfers between devices, shards(): odd_in = lax.ppermute(odd, 'dom', odd_all if section == 0 else odd_fine)  23.8 us
    pallas_call x12, Pallas kernels, call(): pl.pallas_call(kernel, in_specs=[S] * scalars + [place or V] * (inputs -...  17.3 us
    ppermute x4, starting transfers between devices, shards(): even_in = lax.ppermute(even, 'dom', even_all if section == 0 else even_fine)  7.68 us
    ppermute x4, waiting for transfers between devices, shards(): odd_in = lax.ppermute(odd, 'dom', odd_all if section == 0 else odd_fine)  3.85 us
    ppermute x1, starting transfers between devices, shards(): early = lax.ppermute(early, 'dom', down)  1.42 us
    ppermute x1, starting transfers between devices, shards(): late = lax.ppermute(results[1], 'dom', down)  1.29 us
    ppermute x1, starting transfers between devices, shards(): arrived = lax.ppermute(total, 'dom', up)  1.29 us
  transfers between devices with their start and end apart: 11, of which 2 were waited for; matrix products, arithmetic and copies ran while one was open for 0% of the time, Pallas kernels for 19%

profile of v1, /device:TPU:64, one launch (start us, length us, event | category | flops | bytes accessed | tf_op | source)
XLA Modules:
  0.0 58.5 jit_solution(11294385887203837700)
XLA Ops:
  0.8 1.4 %collective-permute-start.2 = (f32[112,128]{1,0:T(8,128)S(1)}, f32[112,128]{1,0:T(8,128)S(1)}, u32[]{:S(2)}, u32[]{:S(2)}) collective-permute-start(f32[112,128]{1,0:T(8,128)S(1)} %get-tuple-element.60), channel_id=1, source_target_pairs={{171,0},{172,1},{173,2},{174,3},{175,4},{176,5},{177,6},{178,7},{1... | collective-permute-start | bytes 172040 | tf_op jit(solution)/shard_map/ppermute | solution.py:695
  2.3 0.7 %setup.1 = (bf16[1024,512]{1,0:T(8,128)(2,1)S(1)}, f32[48,512]{1,0:T(8,128)S(1)}, f32[144,128]{1,0:T(8,128)S(1)}) custom-call(s32[1]{0:T(128)} %bitcast.own_ref, f32[9,3,9]{2,1,0:T(4,128)S(1)} %bitcast.19, f32[3,56,56]{2,1,0:T(8,128)S(1)} %copy-done, f32[9,9]{1,0:T(8,128)S(1)} %copy-done.4, f32[1,128]{1,0:T(1,128)S(1)} %bitcast.23), custom_call_target="tpu_custom_call" | custom-call | flops 20000000 | bytes 2000000 | tf_op jit(solution)/shard_map/setup/pallas_call | solution.py:625
  3.0 2.0 %first.1 = (f32[56,1152]{1,0:T(8,128)S(1)}, f32[56,1152]{1,0:T(8,128)S(1)}, f32[56,1152]{1,0:T(8,128)S(1)}, f32[256,128]{1,0:T(8,128)S(1)}, f32[256,128]{1,0:T(8,128)S(1)}) custom-call(s32[1]{0:T(128)} %bitcast.own_ref, f32[1]{0:T(128)} %bitcast.11.dt_ref, f32[144,128]{1,0:T(8,128)S(1)} %get-tuple-element.44.table_ref, f32[9,56,128]{2,1,0:T(8,128)S(1)} %bitcast.17, ...), custom_call_target="tpu_custom_call" | custom-call | flops 2000000000 | bytes 2000000 | tf_op jit(solution)/shard_map/first/pallas_call | solution.py:625
  5.0 6.1 %collective-permute-start = (f32[256,128]{1,0:T(8,128)S(1)}, f32[256,128]{1,0:T(8,128)S(1)}, u32[]{:S(2)}, u32[]{:S(2)}) collective-permute-start(f32[256,128]{1,0:T(8,128)S(1)} %get-tuple-element.56), channel_id=1, source_target_pairs={{1,2},{3,4},{5,6},{7,8},{9,10},{11,12},{13,14},{15,16},{17,18},{19... | collective-permute-start | bytes 393224 | tf_op jit(solution)/shard_map/ppermute | solution.py:713
  11.2 1.9 %collective-permute-start.1 = (f32[256,128]{1,0:T(8,128)S(1)}, f32[256,128]{1,0:T(8,128)S(1)}, u32[]{:S(2)}, u32[]{:S(2)}) collective-permute-start(f32[256,128]{1,0:T(8,128)S(1)} %get-tuple-element.57), channel_id=1, source_target_pairs={{0,1},{2,3},{4,5},{6,7},{8,9},{10,11},{12,13},{14,15},{16,17},{18,... | collective-permute-start | bytes 393224 | tf_op jit(solution)/shard_map/ppermute | solution.py:714
  13.8 2.0 %prep.1 = (bf16[1024,512]{1,0:T(8,128)(2,1)S(1)}, bf16[1024,512]{1,0:T(8,128)(2,1)S(1)}, bf16[96,192]{1,0:T(8,128)(2,1)S(1)}, bf16[112,192]{1,0:T(8,128)(2,1)S(1...) custom-call(s32[1]{0:T(128)} %bitcast.own_ref, ...), custom_call_target="tpu_custom_call" | custom-call | flops 2000000000 | bytes 2000000 | tf_op jit(solution)/shard_map/prep/pallas_call | solution.py:625
  15.8 1.0 %inner0.1.state_ref = f32[56,1152]{1,0:T(8,128)S(1)} custom-call(s32[1]{0:T(128)} %bitcast.own_ref, f32[56,1152]{1,0:T(8,128)S(1)} %get-tuple-element.46.state_ref, f32[56,1152]{1,0:T(8,128)S(1)} %get-tuple-element.47.w_ref, f32[56,1152]{1,0:T(8,128)S(1)} %get-tuple-element.48.u_ref.sum_in, f32[1,128]{1,0:T(1,128)S(1)} %bitcast.25, ...), custom_call_target="tpu_custom_call" | custom-call | flops 2000000000 | bytes 2000000 | tf_op jit(solution)/shard_map/inner0/pallas_call | solution.py:625
  16.9 2.2 %outer0.1 = (f32[56,1152]{1,0:T(8,128)S(1)}, f32[56,1152]{1,0:T(8,128)S(1)}, f32[56,1152]{1,0:T(8,128)S(1)}, f32[256,128]{1,0:T(8,128)S(1)}, f32[256,128]{1,0:T(8,128)S(1)}, /*index=5*/f32[56,1152]{1,0:T(8,128)S(1)}) custom-call(s32[1]{0:T(128)} %bitcast.own_ref, f32[1]{0:T(128)} %bitcast.13.dt_ref, f32[144,128]{1,0:T(8,128)S(1)} %get-tuple-element.44.table_ref, ...), custom_call_target="tpu_custom_call" | custom-call | flops 2000000000 | bytes 2000000 | tf_op jit(solution)/shard_map/outer0/pallas_call | solution.py:625
  19.1 6.1 %collective-permute-start.3 = (f32[256,128]{1,0:T(8,128)S(1)}, f32[256,128]{1,0:T(8,128)S(1)}, u32[]{:S(2)}, u32[]{:S(2)}) collective-permute-start(f32[256,128]{1,0:T(8,128)S(1)} %get-tuple-element.67), channel_id=1, source_target_pairs={{1,2},{3,4},{5,6},{7,8},{9,10},{11,12},{13,14},{15,16},{17,18},{19... | collective-permute-start | bytes 393224 | tf_op jit(solution)/shard_map/ppermute | solution.py:713
  25.2 1.9 %collective-permute-start.4 = (f32[256,128]{1,0:T(8,128)S(1)}, f32[256,128]{1,0:T(8,128)S(1)}, u32[]{:S(2)}, u32[]{:S(2)}) collective-permute-start(f32[256,128]{1,0:T(8,128)S(1)} %get-tuple-element.68), channel_id=1, source_target_pairs={{0,1},{2,3},{4,5},{6,7},{8,9},{10,11},{12,13},{14,15},{16,17},{18,... | collective-permute-start | bytes 393224 | tf_op jit(solution)/shard_map/ppermute | solution.py:714
  27.2 1.1 %inner1.1 = (f32[56,1152]{1,0:T(8,128)S(1)}, f32[112,128]{1,0:T(8,128)S(1)}) custom-call(s32[1]{0:T(128)} %bitcast.own_ref, f32[56,1152]{1,0:T(8,128)S(1)} %get-tuple-element.62.state_ref.coarse_ref, f32[56,1152]{1,0:T(8,128)S(1)} %get-tuple-element.63.w_ref, f32[56,1152]{1,0:T(8,128)S(1)} %get-tuple-element.64.u_ref, ...), custom_call_target="tpu_custom_call", output_to_operand_aliasing={{1}: (12, {})} | custom-call | flops 2000000000 | bytes 2000000 | tf_op jit(solution)/shard_map/inner1/pallas_call | solution.py:625
  28.3 1.3 %collective-permute-start.5 = (f32[112,128]{1,0:T(8,128)S(1)}, f32[112,128]{1,0:T(8,128)S(1)}, u32[]{:S(2)}, u32[]{:S(2)}) collective-permute-start(f32[112,128]{1,0:T(8,128)S(1)} %get-tuple-element.73), channel_id=1, source_target_pairs={{171,0},{172,1},{173,2},{174,3},{175,4},{176,5},{177,6},{178,7},{1... | collective-permute-start | bytes 172040 | tf_op jit(solution)/shard_map/ppermute | solution.py:753
  29.6 2.1 %outer1.1 = (f32[56,1152]{1,0:T(8,128)S(1)}, f32[56,1152]{1,0:T(8,128)S(1)}, f32[56,1152]{1,0:T(8,128)S(1)}, f32[256,128]{1,0:T(8,128)S(1)}, f32[256,128]{1,0:T(8,128)S(1)}, /*index=5*/f32[56,1152]{1,0:T(8,128)S(1)}) custom-call(s32[1]{0:T(128)} %bitcast.own_ref, f32[1]{0:T(128)} %bitcast.14.dt_ref, f32[144,128]{1,0:T(8,128)S(1)} %get-tuple-element.44.table_ref, ...), custom_call_target="tpu_custom_call" | custom-call | flops 2000000000 | bytes 2000000 | tf_op jit(solution)/shard_map/outer1/pallas_call | solution.py:625
  31.7 6.1 %collective-permute-start.6 = (f32[256,128]{1,0:T(8,128)S(1)}, f32[256,128]{1,0:T(8,128)S(1)}, u32[]{:S(2)}, u32[]{:S(2)}) collective-permute-start(f32[256,128]{1,0:T(8,128)S(1)} %get-tuple-element.74), channel_id=1, source_target_pairs={{1,2},{3,4},{5,6},{7,8},{9,10},{11,12},{13,14},{15,16},{17,18},{19... | collective-permute-start | bytes 393224 | tf_op jit(solution)/shard_map/ppermute | solution.py:713
  37.8 1.9 %collective-permute-start.7 = (f32[256,128]{1,0:T(8,128)S(1)}, f32[256,128]{1,0:T(8,128)S(1)}, u32[]{:S(2)}, u32[]{:S(2)}) collective-permute-start(f32[256,128]{1,0:T(8,128)S(1)} %get-tuple-element.75), channel_id=1, source_target_pairs={{0,1},{2,3},{4,5},{6,7},{8,9},{10,11},{12,13},{14,15},{16,17},{18,... | collective-permute-start | bytes 393224 | tf_op jit(solution)/shard_map/ppermute | solution.py:714
  39.8 1.1 %inner2.1.state_ref = f32[56,1152]{1,0:T(8,128)S(1)} custom-call(s32[1]{0:T(128)} %bitcast.own_ref, f32[56,1152]{1,0:T(8,128)S(1)} %get-tuple-element.70.state_ref, f32[56,1152]{1,0:T(8,128)S(1)} %get-tuple-element.71.w_ref, f32[56,1152]{1,0:T(8,128)S(1)} %get-tuple-element.72.u_ref, f32[1,128]{1,0:T(1,128)S(1)} %bitcast.29, ...), custom_call_target="tpu_custom_call" | custom-call | flops 2000000000 | bytes 2000000 | tf_op jit(solution)/shard_map/inner2/pallas_call | solution.py:625
  40.9 1.9 %collective-permute-done.6.odd_in = f32[256,128]{1,0:T(8,128)S(1)} collective-permute-done((f32[256,128]{1,0:T(8,128)S(1)}, f32[256,128]{1,0:T(8,128)S(1)}, u32[]{:S(2)}, u32[]{:S(2)}) %collective-permute-start.6) | collective-permute-done | bytes 131104 | tf_op jit(solution)/shard_map/ppermute | solution.py:713
  42.8 2.3 %outer2.1 = (f32[56,1152]{1,0:T(8,128)S(1)}, f32[56,1152]{1,0:T(8,128)S(1)}, f32[56,1152]{1,0:T(8,128)S(1)}, f32[256,128]{1,0:T(8,128)S(1)}, f32[256,128]{1,0:T(8,128)S(1)}, /*index=5*/f32[56,128]{1,0:T(8,128)S(1)}) custom-call(s32[1]{0:T(128)} %bitcast.own_ref, f32[1]{0:T(128)} %bitcast.15.dt_ref, f32[144,128]{1,0:T(8,128)S(1)} %get-tuple-element.44.table_ref, ...), custom_call_target="tpu_custom_call" | custom-call | flops 2000000000 | bytes 2000000 | tf_op jit(solution)/shard_map/outer2/pallas_call | solution.py:625
  45.1 1.3 %collective-permute-start.10 = (f32[56,128]{1,0:T(8,128)S(1)}, f32[56,128]{1,0:T(8,128)S(1)}, u32[]{:S(2)}, u32[]{:S(2)}) collective-permute-start(f32[56,128]{1,0:T(8,128)S(1)} %get-tuple-element.82), channel_id=1, source_target_pairs={{0,171},{1,172},{2,173},{3,174},{4,175},{5,176},{6,177},{7,178},{8... | collective-permute-start | bytes 86024 | tf_op jit(solution)/shard_map/ppermute | solution.py:736
  46.4 5.5 %collective-permute-start.8 = (f32[256,128]{1,0:T(8,128)S(1)}, f32[256,128]{1,0:T(8,128)S(1)}, u32[]{:S(2)}, u32[]{:S(2)}) collective-permute-start(f32[256,128]{1,0:T(8,128)S(1)} %get-tuple-element.80), channel_id=1, source_target_pairs={{1,2},{3,4},{5,6},{7,8},{9,10},{11,12},{13,14},{15,16},{17,18},{19... | collective-permute-start | bytes 393224 | tf_op jit(solution)/shard_map/ppermute | solution.py:713
  51.9 1.9 %collective-permute-start.9 = (f32[256,128]{1,0:T(8,128)S(1)}, f32[256,128]{1,0:T(8,128)S(1)}, u32[]{:S(2)}, u32[]{:S(2)}) collective-permute-start(f32[256,128]{1,0:T(8,128)S(1)} %get-tuple-element.81), channel_id=1, source_target_pairs={{0,1},{2,3},{4,5},{6,7},{8,9},{10,11},{12,13},{14,15},{16,17},{18,... | collective-permute-start | bytes 393224 | tf_op jit(solution)/shard_map/ppermute | solution.py:714
  53.8 1.2 %inner3.1.fine_ref = f32[56,1152]{1,0:T(8,128)S(1)} custom-call(s32[1]{0:T(128)} %bitcast.own_ref, f32[56,1152]{1,0:T(8,128)S(1)} %get-tuple-element.77.state_ref, f32[56,1152]{1,0:T(8,128)S(1)} %get-tuple-element.78.w_ref, f32[56,1152]{1,0:T(8,128)S(1)} %get-tuple-element.79.u_ref, f32[1,128]{1,0:T(1,128)S(1)} %bitcast.31, ...), custom_call_target="tpu_custom_call" | custom-call | flops 2000000000 | bytes 2000000 | tf_op jit(solution)/shard_map/inner3/pallas_call | solution.py:625
  55.0 1.9 %collective-permute-done.8.odd_in = f32[256,128]{1,0:T(8,128)S(1)} collective-permute-done((f32[256,128]{1,0:T(8,128)S(1)}, f32[256,128]{1,0:T(8,128)S(1)}, u32[]{:S(2)}, u32[]{:S(2)}) %collective-permute-start.8) | collective-permute-done | bytes 131104 | tf_op jit(solution)/shard_map/ppermute | solution.py:713
  56.9 1.5 %last.1 = f32[9,56,128]{2,1,0:T(8,128)} custom-call(s32[1]{0:T(128)} %bitcast.own_ref, f32[56,1152]{1,0:T(8,128)S(1)} %inner3.1.fine_ref, f32[56,1152]{1,0:T(8,128)S(1)} %get-tuple-element.62.state_ref.coarse_ref, f32[256,128]{1,0:T(8,128)S(1)} %collective-permute-done.8.odd_in, f32[256,128]{1,0:T(8,128)S(1)} %collective-permute-done.9.even_in, ...), custom_call_target="tpu_custom_call" | custom-call | flops 1000000000 | bytes 2000000 | tf_op jit(solution)/shard_map/last/pallas_call | solution.py:625
  (34 shorter events, 0.8 us)
Async XLA Ops:
  0.7 1.6 %copy-start = (f32[3,56,56]{2,1,0:T(8,128)S(1)}, f32[3,56,56]{2,1,0:T(8,128)}, u32[]{:S(2)}) copy-start(f32[3,56,56]{2,1,0:T(8,128)} %stiff_ref.3) | copy-start | bytes 112900
  0.7 1.6 %copy-start.2 = (f32[3,9,9]{2,0,1:T(4,128)S(1)}, f32[3,9,9]{2,0,1:T(4,128)}, u32[]{:S(2)}) copy-start(f32[3,9,9]{2,0,1:T(4,128)} %param.17) | copy-start | bytes 2920
  0.7 1.6 %copy-start.4 = (f32[9,9]{1,0:T(8,128)S(1)}, f32[9,9]{1,0:T(8,128)}, u32[]{:S(2)}) copy-start(f32[9,9]{1,0:T(8,128)} %refs_2_.1) | copy-start | bytes 976
  0.7 2.3 %copy-start.1 = (f32[56,9,128]{2,0,1:T(8,128)S(1)}, f32[56,9,128]{2,0,1:T(8,128)}, u32[]{:S(2)}) copy-start(f32[56,9,128]{2,0,1:T(8,128)} %param.13) | copy-start | bytes 774148
  0.8 1.5 %copy-start.5 = (f32[128]{0:T(128)S(1)}, f32[128]{0:T(128)}, u32[]{:S(2)}) copy-start(f32[128]{0:T(128)} %param.14) | copy-start | bytes 1540
  0.8 16.1 %collective-permute-start.2 = (f32[112,128]{1,0:T(8,128)S(1)}, f32[112,128]{1,0:T(8,128)S(1)}, u32[]{:S(2)}, u32[]{:S(2)}) collective-permute-start(f32[112,128]{1,0:T(8,128)S(1)} %get-tuple-element.60), channel_id=1, source_target_pairs={{171,0},{172,1},{173,2},{174,3},{175,4},{176,5},{177,6},{178,7},{1... | collective-permute-start | bytes 172040 | tf_op jit(solution)/shard_map/ppermute | solution.py:695
  3.0 10.1 %copy-start.3 = (f32[4,21,56]{2,0,1:T(4,128)S(1)}, f32[4,21,56]{2,0,1:T(4,128)}, u32[]{:S(2)}) copy-start(f32[4,21,56]{2,0,1:T(4,128)} %param.18) | copy-start | bytes 56452
  3.0 10.1 %copy-start.8 = (f32[4,56,21]{1,0,2:T(4,128)S(1)}, f32[4,56,21]{1,0,2:T(4,128)}, u32[]{:S(2)}) copy-start(f32[4,56,21]{1,0,2:T(4,128)} %param.19) | copy-start | bytes 56452
  3.0 10.1 %copy-start.10 = (s32[4,128]{1,0:T(4,128)S(1)}, s32[4,128]{1,0:T(4,128)}, u32[]{:S(2)}) copy-start(s32[4,128]{1,0:T(4,128)} %face_ref.1) | copy-start | bytes 6148
  3.0 10.1 %copy-start.11 = (s32[256]{0:T(256)S(1)}, s32[256]{0:T(256)}, u32[]{:S(2)}) copy-start(s32[256]{0:T(256)} %param.25) | copy-start | bytes 3076
  5.0 11.8 %collective-permute-start = (f32[256,128]{1,0:T(8,128)S(1)}, f32[256,128]{1,0:T(8,128)S(1)}, u32[]{:S(2)}, u32[]{:S(2)}) collective-permute-start(f32[256,128]{1,0:T(8,128)S(1)} %get-tuple-element.56), channel_id=1, source_target_pairs={{1,2},{3,4},{5,6},{7,8},{9,10},{11,12},{13,14},{15,16},{17,18},{19... | collective-permute-start | bytes 393224 | tf_op jit(solution)/shard_map/ppermute | solution.py:713
  11.2 5.7 %collective-permute-start.1 = (f32[256,128]{1,0:T(8,128)S(1)}, f32[256,128]{1,0:T(8,128)S(1)}, u32[]{:S(2)}, u32[]{:S(2)}) collective-permute-start(f32[256,128]{1,0:T(8,128)S(1)} %get-tuple-element.57), channel_id=1, source_target_pairs={{0,1},{2,3},{4,5},{6,7},{8,9},{10,11},{12,13},{14,15},{16,17},{18,... | collective-permute-start | bytes 393224 | tf_op jit(solution)/shard_map/ppermute | solution.py:714
  13.1 0.7 %copy-start.9 = (s32[4,128]{1,0:T(4,128)S(1)}, s32[4,128]{1,0:T(4,128)}, u32[]{:S(2)}) copy-start(s32[4,128]{1,0:T(4,128)} %index_ref.1) | copy-start | bytes 6148
  13.1 0.7 %copy-start.6 = (s32[32]{0:T(128)S(1)}, s32[32]{0:T(128)}, u32[]{:S(2)}) copy-start(s32[32]{0:T(128)} %param.23) | copy-start | bytes 388
  13.1 0.7 %copy-start.7 = (s32[32]{0:T(128)S(1)}, s32[32]{0:T(128)}, u32[]{:S(2)}) copy-start(s32[32]{0:T(128)} %param.24) | copy-start | bytes 388
  19.1 10.5 %collective-permute-start.3 = (f32[256,128]{1,0:T(8,128)S(1)}, f32[256,128]{1,0:T(8,128)S(1)}, u32[]{:S(2)}, u32[]{:S(2)}) collective-permute-start(f32[256,128]{1,0:T(8,128)S(1)} %get-tuple-element.67), channel_id=1, source_target_pairs={{1,2},{3,4},{5,6},{7,8},{9,10},{11,12},{13,14},{15,16},{17,18},{19... | collective-permute-start | bytes 393224 | tf_op jit(solution)/shard_map/ppermute | solution.py:713
  25.2 4.4 %collective-permute-start.4 = (f32[256,128]{1,0:T(8,128)S(1)}, f32[256,128]{1,0:T(8,128)S(1)}, u32[]{:S(2)}, u32[]{:S(2)}) collective-permute-start(f32[256,128]{1,0:T(8,128)S(1)} %get-tuple-element.68), channel_id=1, source_target_pairs={{0,1},{2,3},{4,5},{6,7},{8,9},{10,11},{12,13},{14,15},{16,17},{18,... | collective-permute-start | bytes 393224 | tf_op jit(solution)/shard_map/ppermute | solution.py:714
  28.3 11.4 %collective-permute-start.5 = (f32[112,128]{1,0:T(8,128)S(1)}, f32[112,128]{1,0:T(8,128)S(1)}, u32[]{:S(2)}, u32[]{:S(2)}) collective-permute-start(f32[112,128]{1,0:T(8,128)S(1)} %get-tuple-element.73), channel_id=1, source_target_pairs={{171,0},{172,1},{173,2},{174,3},{175,4},{176,5},{177,6},{178,7},{1... | collective-permute-start | bytes 172040 | tf_op jit(solution)/shard_map/ppermute | solution.py:753
  31.7 11.1 %collective-permute-start.6 = (f32[256,128]{1,0:T(8,128)S(1)}, f32[256,128]{1,0:T(8,128)S(1)}, u32[]{:S(2)}, u32[]{:S(2)}) collective-permute-start(f32[256,128]{1,0:T(8,128)S(1)} %get-tuple-element.74), channel_id=1, source_target_pairs={{1,2},{3,4},{5,6},{7,8},{9,10},{11,12},{13,14},{15,16},{17,18},{19... | collective-permute-start | bytes 393224 | tf_op jit(solution)/shard_map/ppermute | solution.py:713
  37.8 5.0 %collective-permute-start.7 = (f32[256,128]{1,0:T(8,128)S(1)}, f32[256,128]{1,0:T(8,128)S(1)}, u32[]{:S(2)}, u32[]{:S(2)}) collective-permute-start(f32[256,128]{1,0:T(8,128)S(1)} %get-tuple-element.75), channel_id=1, source_target_pairs={{0,1},{2,3},{4,5},{6,7},{8,9},{10,11},{12,13},{14,15},{16,17},{18,... | collective-permute-start | bytes 393224 | tf_op jit(solution)/shard_map/ppermute | solution.py:714
  45.1 9.9 %collective-permute-start.10 = (f32[56,128]{1,0:T(8,128)S(1)}, f32[56,128]{1,0:T(8,128)S(1)}, u32[]{:S(2)}, u32[]{:S(2)}) collective-permute-start(f32[56,128]{1,0:T(8,128)S(1)} %get-tuple-element.82), channel_id=1, source_target_pairs={{0,171},{1,172},{2,173},{3,174},{4,175},{5,176},{6,177},{7,178},{8... | collective-permute-start | bytes 86024 | tf_op jit(solution)/shard_map/ppermute | solution.py:736
  46.4 10.5 %collective-permute-start.8 = (f32[256,128]{1,0:T(8,128)S(1)}, f32[256,128]{1,0:T(8,128)S(1)}, u32[]{:S(2)}, u32[]{:S(2)}) collective-permute-start(f32[256,128]{1,0:T(8,128)S(1)} %get-tuple-element.80), channel_id=1, source_target_pairs={{1,2},{3,4},{5,6},{7,8},{9,10},{11,12},{13,14},{15,16},{17,18},{19... | collective-permute-start | bytes 393224 | tf_op jit(solution)/shard_map/ppermute | solution.py:713
  51.9 5.0 %collective-permute-start.9 = (f32[256,128]{1,0:T(8,128)S(1)}, f32[256,128]{1,0:T(8,128)S(1)}, u32[]{:S(2)}, u32[]{:S(2)}) collective-permute-start(f32[256,128]{1,0:T(8,128)S(1)} %get-tuple-element.81), channel_id=1, source_target_pairs={{0,1},{2,3},{4,5},{6,7},{8,9},{10,11},{12,13},{14,15},{16,17},{18,... | collective-permute-start | bytes 393224 | tf_op jit(solution)/shard_map/ppermute | solution.py:714
